TPU v7x, 32 devices: a whole 2x2x4 slice. The times are simulated.
32 devices in a mesh: mem: 4 (over x, core), wide: 8 (over z, y).
Axes of the slice: x: 2, y: 2, z: 4, core: 2. Of those that a mesh axis runs over, the one named last changes fastest.
Arguments:
- control: float32 [8, 64, 128, 720], P('mem', 'wide'), may hold values from -6 to 6
- perturb: float32 [8, 3, 64, 128, 720], P('mem', None, None, 'wide'), may hold values from -6 to 6
- obs_count: int32 [128, 720], P('wide'), may hold values from 0 to 3
- obs_kind: int32 [128, 720], P('wide'), may hold values from 0 to 7
- obs_table: float32 [8, 192], replicated, may hold values from 0.25 to 4
- band_filter: float32 [64, 64], replicated, may hold values from -0.9 to 1.2, as said below
- diffusivity: float32 [128, 720], replicated, may hold values from 0.04 to 0.24
Outputs:
- hessian_product: float32 [8, 64, 128, 720], P('mem', 'wide')
Inputs may be any that keep to these rules, and one draw needn't show every extreme that they name: band_filter[i, j] is zero where |i - j| > 4; its diagonal lies between 0.8 and 1.2.
All inputs are finite; a program needn't handle non-finite values.
Results may differ from a plain program's by a relative error of at most 0.00005.
Values sent between devices are 32-bit elements; how exact they have to be, the bound alone decides.
A program may use at most 128 MiB of HBM per device.

v0:
```python
import jax
import jax.numpy as jnp
from jax import lax
from jax.sharding import PartitionSpec as P

ITERS = 16


def edge_coeffs(diffusivity):
    east_edge = 0.5 * (diffusivity + jnp.roll(diffusivity, -1, axis=1))
    north_edge = 0.5 * (diffusivity + jnp.roll(diffusivity, -1, axis=0))
    row_index = lax.broadcasted_iota(jnp.int32, diffusivity.shape, 0)
    north_edge = jnp.where(
        row_index < diffusivity.shape[0] - 1, north_edge, jnp.zeros_like(north_edge)
    )
    return (east_edge, north_edge)


def diffuse(field, east_edge, north_edge):

    def one_step(step_index, field_now):
        flux_east = east_edge * (jnp.roll(field_now, -1, axis=-1) - field_now)
        flux_north = north_edge * (jnp.roll(field_now, -1, axis=-2) - field_now)
        increment_field = (
            flux_east
            - jnp.roll(flux_east, 1, axis=-1)
            + flux_north
            - jnp.roll(flux_north, 1, axis=-2)
        )
        return field_now + increment_field

    return lax.fori_loop(0, ITERS, one_step, field)


def weights_for(cell_count, kind_of_cell, table_levels):
    kind_rows = lax.broadcasted_iota(jnp.int32, (table_levels.shape[0],) + kind_of_cell.shape, 0)
    one_hot = (kind_of_cell[None, :, :] == kind_rows).astype(jnp.float32)
    looked_up = jnp.einsum("kvl,kij->vlij", table_levels, one_hot, precision=lax.Precision.HIGHEST)
    return looked_up * cell_count.astype(jnp.float32)[None, None, :, :]


def local(control, perturb, obs_count, obs_kind, obs_table, band_filter, diffusivity):
    highest_level = lax.Precision.HIGHEST
    mem_dev, lev_dev, nlat, nlon = control.shape
    levels = perturb.shape[2]
    east_edge, north_edge = edge_coeffs(diffusivity)
    table_levels = obs_table.reshape(obs_table.shape[0], 3, levels)
    partial_accumulated_sum = jnp.zeros(perturb.shape[1:], jnp.float32)
    for member in range(mem_dev):
        smooth = diffuse(control[member : member + 1], east_edge, north_edge)
        columns = lax.all_to_all(smooth, "wide", split_axis=2, concat_axis=1, tiled=True)
        filtered_field = jnp.einsum("lm,kmij->klij", band_filter, columns, precision=highest_level)
        partial_accumulated_sum = partial_accumulated_sum + jnp.einsum(
            "kvlij,klij->vlij",
            perturb[member : member + 1],
            filtered_field,
            precision=highest_level,
        )
    total_sum = lax.psum(partial_accumulated_sum, "mem")
    weighted_field = weights_for(obs_count, obs_kind, table_levels) * total_sum
    adjoint_field = jnp.einsum("kvlij,vlij->klij", perturb, weighted_field, precision=highest_level)
    lifted = jnp.einsum("lm,klij->kmij", band_filter, adjoint_field, precision=highest_level)
    results = []
    for member in range(mem_dev):
        member_plane = lax.all_to_all(
            lifted[member : member + 1], "wide", split_axis=1, concat_axis=2, tiled=True
        )
        results.append(diffuse(member_plane, east_edge, north_edge))
    spread = jnp.concatenate(results, axis=0)
    return control + spread


def solution(mesh):
    placed = (
        P("mem", "wide", None, None),
        P("mem", None, None, "wide", None),
        P("wide", None),
        P("wide", None),
        P(),
        P(),
        P(),
    )
    return jax.shard_map(
        local, mesh=mesh, in_specs=placed, out_specs=P("mem", "wide", None, None), check_vma=False
    )
```

profile of v0, /device:TPU:0, one launch (start us, length us, event | category | flops | bytes accessed | tf_op | source)
XLA Modules:
  0.0 817.8 jit_solution(14129425184466669537)
XLA Ops:
  10.2 5.7 fusion.55
  20.5 89.4 %while.40 = (s32[]{:T(128)}, f32[1,8,128,720]{3,2,1,0:T(8,128)S(1)}, f32[128,720]{1,0:T(8,128)}, f32[128,720]{1,0:T(8,128)}, s32[]{:T(128)}) while((s32[]{:T(128)}, f32[1,8,128,720]{3,2,1,0:T(8,128)S(1)}, f32[128,720]{1,0:T(8,128)}, f32[128,720]{1,0:T(8,128)}, s32[]{:T(128)}) %tuple.76), condition=%wide.region_1.2_spmd, body=%wide.region_0.1_spmd.sunk | while | flops 8847362 | bytes 47977588 | solution.py:32
  110.0 3.5 copy.50
  113.4 7.5 all-to-all-start
  123.3 89.5 %while.41 = (s32[]{:T(128)}, f32[1,8,128,720]{3,2,1,0:T(8,128)S(1)}, f32[128,720]{1,0:T(8,128)}, f32[128,720]{1,0:T(8,128)}, s32[]{:T(128)}) while((s32[]{:T(128)}, f32[1,8,128,720]{3,2,1,0:T(8,128)S(1)}, f32[128,720]{1,0:T(8,128)}, f32[128,720]{1,0:T(8,128)}, s32[]{:T(128)}) %tuple.92), condition=%wide.region_3.4_spmd, body=%wide.region_2.3_spmd.sunk | while | flops 8847362 | bytes 47977588 | solution.py:32
  212.8 3.5 copy.54
  216.3 6.0 all-to-all-start.1
  222.7 11.8 %fusion.53 = (f32[1,3,64,16,720]{4,3,2,1,0:T(8,128)}, f32[1,3,64,16,720]{4,3,2,1,0:T(8,128)}) fusion(f32[2,3,64,16,720]{4,3,2,1,0:T(8,128)} %param.16), kind=kLoop, calls=%fused_computation.67 | loop fusion | bytes 35389440 | tf_op jit(solution)/shard_map/slice | solution.py:55
  234.5 4.9 fusion.36
  239.4 53.1 %all-to-all-done.1 = f32[1,8,128,720]{3,1,0,2:T(8,128)} async-done(((f32[1,8,128,720]{3,1,0,2:T(8,128)}), f32[1,8,128,720]{3,1,0,2:T(8,128)}, u32[]{:S(2)}, u32[]{:S(2)}) %all-to-all-start.1) | async-done | bytes 2949152 | tf_op jit(solution)/shard_map/all_to_all | solution.py:51
  292.6 5.0 fusion.39
  297.6 20.1 %fusion.21 = f32[3,64,16,720]{3,1,0,2:T(8,128)} fusion(f32[1,3,64,16,720]{4,3,2,1,0:T(8,128)} %get-tuple-element.138, f32[1,3,64,16,720]{4,3,2,1,0:T(8,128)} %get-tuple-element.137, f32[64,16,720]{2,0,1:T(8,128)S(1)} %fusion.39, f32[64,16,720]{2,0,1:T(8,128)S(1)} %fusion.36), kind=kLoop, calls=%fused_computation.35 | loop fusion | flops 6635520 | bytes 32440320 | tf_op jit(solution)/shard_map/add | solution.py:53
  318.6 168.2 %all-reduce.2.cloned.1.call-done = f32[3,64,16,720]{3,1,0,2:T(8,128)} async-done(((f32[3,64,16,720]{3,1,0,2:T(8,128)}), f32[3,64,16,720]{3,1,0,2:T(8,128)}) %all-reduce.2.cloned.1.call-update) | async-done | bytes 8847376 | tf_op jit(solution)/shard_map/psum | solution.py:59
  486.8 9.3 %fusion.23 = f32[64,16,720,3]{2,0,3,1:T(8,128)} fusion(f32[3,64,16,720]{3,1,0,2:T(8,128)} %all-reduce.2.cloned.1.call-done, f32[16,720]{1,0:T(8,128)S(1)} %convert_element_type.4, s32[16,720]{1,0:T(8,128)S(1)} %copy-done.12, f32[8,3,64]{2,1,0:T(4,128)S(1)} %reshape.47), kind=kOutput, calls=%fused_computation.39 | convolution fusion | flops 216852480 | bytes 17793024 | tf_op jit(solution)/shard_map/kvl,kij->vlij/dot_general | solution.py:38
  496.1 13.1 %copy.79 = f32[64,16,720,3]{2,1,0,3:T(8,128)} copy(f32[64,16,720,3]{2,0,3,1:T(8,128)} %fusion.23) | data formatting | bytes 17694720
  509.3 7.1 multiply_reduce_fusion
  516.4 10.1 %fusion.33 = f32[2,64,16,720]{3,1,2,0:T(8,128)S(1)} fusion(f32[64,16,720,2]{2,1,0,3:T(8,128)S(1)} %multiply_reduce_fusion, f32[64,64]{1,0:T(8,128)S(1)} %copy-done), kind=kOutput, calls=%fused_computation.50 | convolution fusion | flops 1132462080 | bytes 11812864 | tf_op jit(solution)/shard_map/lm,klij->kmij/dot_general | solution.py:62
  528.8 3.5 copy.58
  532.3 5.8 all-to-all-start.2
  538.1 5.4 copy.60
  543.5 65.1 %all-to-all-done.2 = f32[1,64,16,720]{3,2,0,1:T(8,128)S(1)} async-done(((f32[1,64,16,720]{3,2,0,1:T(8,128)}), f32[1,64,16,720]{3,2,0,1:T(8,128)S(1)}, u32[]{:S(2)}, u32[]{:S(2)}) %all-to-all-start.2) | async-done | bytes 2949152 | tf_op jit(solution)/shard_map/all_to_all | solution.py:65
  610.3 4.4 all-to-all-start.3
  616.9 89.6 %while.42 = (s32[]{:T(128)}, f32[1,8,128,720]{3,2,1,0:T(8,128)S(1)}, f32[128,720]{1,0:T(8,128)}, f32[128,720]{1,0:T(8,128)}, s32[]{:T(128)}) while((s32[]{:T(128)}, f32[1,8,128,720]{3,2,1,0:T(8,128)S(1)}, f32[128,720]{1,0:T(8,128)}, f32[128,720]{1,0:T(8,128)}, s32[]{:T(128)}) %tuple.93), condition=%wide.region_6.7_spmd, body=%wide.region_5.6_spmd.sunk | while | flops 8847362 | bytes 47977588 | solution.py:32
  620.1 2.4 fusion.69
  625.7 2.4 fusion.69
  631.3 2.4 fusion.69
  636.9 2.4 fusion.69
  642.5 2.4 fusion.69
  648.1 2.4 fusion.69
  653.7 2.4 fusion.69
  659.3 2.4 fusion.69
  664.9 2.4 fusion.69
  670.5 2.4 fusion.69
  676.1 2.4 fusion.69
  681.7 2.4 fusion.69
  687.3 2.4 fusion.69
  711.1 89.6 %while.43 = (s32[]{:T(128)}, f32[1,8,128,720]{3,2,1,0:T(8,128)S(1)}, f32[128,720]{1,0:T(8,128)}, f32[128,720]{1,0:T(8,128)}, s32[]{:T(128)}) while((s32[]{:T(128)}, f32[1,8,128,720]{3,2,1,0:T(8,128)S(1)}, f32[128,720]{1,0:T(8,128)}, f32[128,720]{1,0:T(8,128)}, s32[]{:T(128)}) %tuple.94), condition=%wide.region_8.9_spmd, body=%wide.region_7.8_spmd.sunk | while | flops 8847362 | bytes 47977588 | solution.py:32
  714.2 2.4 fusion.71
  719.8 2.4 fusion.71
  725.4 2.4 fusion.71
  731.0 2.4 fusion.71
  753.4 2.4 fusion.71
  759.0 2.4 fusion.71
  764.6 2.4 fusion.71
  770.2 2.4 fusion.71
  775.8 2.4 fusion.71
  781.4 2.4 fusion.71
  803.0 7.6 maximum_add_fusion
  (792 shorter events, 322.4 us)
Async XLA Ops:
  6.5 228.0 %copy-start = (f32[64,64]{1,0:T(8,128)S(1)}, f32[64,64]{1,0:T(8,128)}, u32[]{:S(2)}) copy-start(f32[64,64]{1,0:T(8,128)} %param.20) | copy-start | bytes 49156
  7.7 8.2 %copy-start.11 = (f32[128,720]{1,0:T(8,128)}, f32[128,720]{1,0:T(8,128)S(1)}, u32[]{:S(2)}) copy-start(f32[128,720]{1,0:T(8,128)S(1)} %copy.46) | copy-start | bytes 1105924
  15.9 2.4 slice-start.5
  21.4 1.1 copy-start.6
  27.0 1.1 copy-start.6
  32.6 1.1 copy-start.6
  38.2 1.1 copy-start.6
  43.8 1.1 copy-start.6
  49.4 1.1 copy-start.6
  55.0 1.1 copy-start.6
  60.5 1.1 copy-start.6
  71.7 1.1 copy-start.6
  77.3 1.1 copy-start.6
  82.9 1.1 copy-start.6
  88.5 1.1 copy-start.6
  94.1 1.1 copy-start.6
  99.7 1.1 copy-start.6
  105.3 1.1 copy-start.6
  113.4 102.9 %all-to-all-start = ((f32[1,8,128,720]{3,1,0,2:T(8,128)}), f32[1,8,128,720]{3,1,0,2:T(8,128)}, u32[]{:S(2)}, u32[]{:S(2)}) async-start(f32[1,8,128,720]{3,1,0,2:T(8,128)} %copy.50), calls=%async_computation | async-start | bytes 6291456 | tf_op jit(solution)/shard_map/all_to_all | solution.py:51
  124.2 1.1 copy-start.7
  129.8 1.1 copy-start.7
  135.4 1.1 copy-start.7
  141.0 1.1 copy-start.7
  146.6 1.1 copy-start.7
  152.2 1.1 copy-start.7
  157.8 1.1 copy-start.7
  163.4 1.1 copy-start.7
  169.0 1.1 copy-start.7
  174.6 1.1 copy-start.7
  180.1 1.1 copy-start.7
  185.7 1.1 copy-start.7
  191.3 1.1 copy-start.7
  196.9 1.1 copy-start.7
  202.5 1.1 copy-start.7
  208.1 1.1 copy-start.7
  216.3 76.3 %all-to-all-start.1 = ((f32[1,8,128,720]{3,1,0,2:T(8,128)}), f32[1,8,128,720]{3,1,0,2:T(8,128)}, u32[]{:S(2)}, u32[]{:S(2)}) async-start(f32[1,8,128,720]{3,1,0,2:T(8,128)} %copy.54), calls=%async_computation.1 | async-start | bytes 6291456 | tf_op jit(solution)/shard_map/all_to_all | solution.py:51
  222.3 264.5 %all-reduce.2.cloned.1.call-start = ((), (), s32[]{:S(2)}) async-start(), calls=%async_computation.4 | async-start | bytes 18874368 | tf_op jit(solution)/shard_map/psum | solution.py:59
  317.7 169.1 %copy-start.12 = (s32[16,720]{1,0:T(8,128)S(1)}, s32[16,720]{1,0:T(8,128)}, u32[]{:S(2)}) copy-start(s32[16,720]{1,0:T(8,128)} %param.18) | copy-start | bytes 138244
  486.8 22.5 %slice-start = ((s8[18874368]{0:T(1024)(128)(4,1)}), s8[4194304]{0:T(1024)(128)(4,1)S(1)}, s32[]{:S(2)}) async-start(s8[18874368]{0:T(1024)(128)(4,1)} %bitcast.113), calls=%async_computation.5 | async-start | bytes 8388608
  486.8 22.5 %slice-start.1 = ((s8[18874368]{0:T(1024)(128)(4,1)}), s8[4194304]{0:T(1024)(128)(4,1)S(1)}, s32[]{:S(2)}) async-start(s8[18874368]{0:T(1024)(128)(4,1)} %bitcast.113), calls=%async_computation.6 | async-start | bytes 8388608
  486.8 22.5 %slice-start.2 = ((s8[18874368]{0:T(1024)(128)(4,1)}), s8[4194304]{0:T(1024)(128)(4,1)S(1)}, s32[]{:S(2)}) async-start(s8[18874368]{0:T(1024)(128)(4,1)} %bitcast.113), calls=%async_computation.7 | async-start | bytes 8388608
  496.1 13.1 %slice-start.3 = ((s8[18874368]{0:T(1024)(128)(4,1)}), s8[4194304]{0:T(1024)(128)(4,1)S(1)}, s32[]{:S(2)}) async-start(s8[18874368]{0:T(1024)(128)(4,1)} %bitcast.113), calls=%async_computation.8 | async-start | bytes 8388608
  496.1 13.1 %slice-start.4 = ((s8[18874368]{0:T(1024)(128)(4,1)}), s8[2097152]{0:T(1024)(128)(4,1)S(1)}, s32[]{:S(2)}) async-start(s8[18874368]{0:T(1024)(128)(4,1)} %bitcast.113), calls=%async_computation.9 | async-start | bytes 4194304
  532.3 76.3 %all-to-all-start.2 = ((f32[1,64,16,720]{3,2,0,1:T(8,128)}), f32[1,64,16,720]{3,2,0,1:T(8,128)S(1)}, u32[]{:S(2)}, u32[]{:S(2)}) async-start(f32[1,64,16,720]{3,2,0,1:T(8,128)} %copy.58), calls=%async_computation.2 | async-start | bytes 6291456 | tf_op jit(solution)/shard_map/all_to_all | solution.py:65
  608.6 1.7 copy-start.10
  610.3 98.6 %all-to-all-start.3 = ((f32[1,64,16,720]{3,2,0,1:T(8,128)}), f32[1,64,16,720]{3,2,0,1:T(8,128)}, u32[]{:S(2)}, u32[]{:S(2)}) async-start(f32[1,64,16,720]{3,2,0,1:T(8,128)} %copy.60), calls=%async_computation.3 | async-start | bytes 6291456 | tf_op jit(solution)/shard_map/all_to_all | solution.py:65
  617.8 1.1 copy-start.8
  803.0 7.6 copy-start.1
  (98 other events, 101.2 us)
Sparse Core Ops, SparseCore 0:
  317.9 168.8 all-reduce.1
where the time goes:
time: 826 us; the launch traced here: 818 us
  waiting for transfers between devices  286 us (35%)
  other arithmetic  251 us (30%)
  local copies, waits for them, and re-layouts  208 us (25%)
  matrix products  29.3 us (4%)
  starting transfers between devices  24.2 us (3%)
  between operations  14.1 us (2%)
    psum x1, waiting for transfers between devices, local(): total_sum = lax.psum(partial_accumulated_sum, 'mem')  168 us
    add x64, other arithmetic, one_step(): return field_now + increment_field  155 us
    all_to_all x2, waiting for transfers between devices, local(): lax.all_to_all(lifted[member:member + 1], 'wide', split_axis=1, concat_ax...  65.1 us
    mul x64, other arithmetic, one_step(): flux_east = east_edge * (jnp.roll(field_now, -1, axis=-1) - field_now)  58.8 us
    slice x128, local copies, waits for them, and re-layouts, one_step(): flux_east = east_edge * (jnp.roll(field_now, -1, axis=-1) - field_now)  58.2 us
    all_to_all x2, waiting for transfers between devices, local(): lax.all_to_all(smooth, 'wide', split_axis=2, concat_axis=1, tiled=True)  53.1 us
    while x256, local copies, waits for them, and re-layouts  50.3 us
    unnamed x28, local copies, waits for them, and re-layouts  21.4 us
  transfers between devices with their start and end apart: 5, of which 3 were waited for; matrix products, arithmetic and copies ran while one was open for 22% of the time, Pallas kernels for 0%

commit v1 on v0

v1 whole, which is shorter than its diff:
```python
import functools

import jax
import jax.numpy as jnp
from jax import lax
from jax.experimental import pallas as pl
from jax.experimental.pallas import tpu as pltpu
from jax.sharding import PartitionSpec as P

ITERS = 16
HB = 4
LANES = 128
VMEM_LIMIT = 48 * 1024 * 1024


def edge_coeffs(diffusivity):
    east_edge = 0.5 * (diffusivity + jnp.roll(diffusivity, -1, axis=1))
    north_edge = 0.5 * (diffusivity + jnp.roll(diffusivity, -1, axis=0))
    row_index = lax.broadcasted_iota(jnp.int32, diffusivity.shape, 0)
    north_edge = jnp.where(
        row_index < diffusivity.shape[0] - 1, north_edge, jnp.zeros_like(north_edge)
    )
    return (east_edge, north_edge)


def strip_rows(count):
    return 8 if count % 8 == 0 else count


def run_steps(nlon, scr, east_ref, north_ref):
    rows = strip_rows(nlon)
    strips = nlon // rows
    nlat = scr.shape[1]
    row_index = lax.broadcasted_iota(jnp.int32, (rows, nlat), 0)
    is_last = row_index == rows - 1
    is_first = row_index == 0

    def one_step(_, carry):
        cur = scr[pl.ds(0, rows), :]
        rot_first = rot_cur = pltpu.roll(cur, rows - 1, 0)
        end = pl.ds((strips - 1) * rows, rows)
        last = scr[end, :]
        beyond = jnp.where(is_last, rot_first, pltpu.roll(last, rows - 1, 0))
        rot_fe_prev = pltpu.roll(east_ref[end, :] * (beyond - last), 1, 0)
        for strip in range(strips):
            here = pl.ds(strip * rows, rows)
            if strip < strips - 1:
                nxt = scr[pl.ds((strip + 1) * rows, rows), :]
                rot_nxt = pltpu.roll(nxt, rows - 1, 0)
            else:
                nxt, rot_nxt = cur, rot_first
            flux_east = east_ref[here, :] * (jnp.where(is_last, rot_nxt, rot_cur) - cur)
            rot_fe = pltpu.roll(flux_east, 1, 0)
            flux_west = jnp.where(is_first, rot_fe_prev, rot_fe)
            flux_north = north_ref[here, :] * (pltpu.roll(cur, nlat - 1, 1) - cur)
            flux_south = pltpu.roll(flux_north, 1, 1)
            scr[here, :] = cur + (flux_east - flux_west + flux_north - flux_south)
            cur, rot_cur, rot_fe_prev = nxt, rot_nxt, rot_fe
        return carry

    lax.fori_loop(0, ITERS, one_step, 0)


def forward_kernel(bounds, chunk, east_ref, north_ref, control_ref, *rest):
    outs, scr = rest[:-1], rest[-1]
    nlon = control_ref.shape[2]
    scr[pl.ds(0, nlon), :] = control_ref[0, 0]
    if scr.shape[0] > nlon:
        scr[pl.ds(nlon, scr.shape[0] - nlon), :] = jnp.zeros(
            (scr.shape[0] - nlon, scr.shape[1]), jnp.float32
        )
    run_steps(nlon, scr, east_ref, north_ref)
    for (start, stop), out in zip(bounds, outs):
        per = out.shape[3]
        turned = scr[pl.ds(start, chunk), :].T
        for dest in range(out.shape[0]):
            out[dest, 0, 0] = turned[dest * per : (dest + 1) * per, : stop - start]


def backward_kernel(bounds, east_ref, north_ref, control_ref, *rest):
    parts, out_ref, scr, turn = rest[:-3], rest[-3], rest[-2], rest[-1]
    nlon = out_ref.shape[2]
    for (start, stop), part in zip(bounds, parts):
        per = part.shape[3]
        for source in range(part.shape[0]):
            turn[pl.ds(source * per, per), pl.ds(0, stop - start)] = part[source, 0, 0]
        scr[pl.ds(start, stop - start), :] = turn[...].T[: stop - start]
    run_steps(nlon, scr, east_ref, north_ref)
    out_ref[0, 0] = control_ref[0, 0] + scr[pl.ds(0, nlon), :]


def window(level, levels):
    return range(max(0, level - HB), min(levels, level + HB + 1))


def increment_kernel(levels, smooth_ref, perturb_ref, band_ref, flag_ref, keep_ref, give_ref):
    mem_dev, variables = perturb_ref.shape[:2]
    per = smooth_ref.shape[2]
    lower_mine = jnp.full(perturb_ref.shape[3:], flag_ref[0], jnp.int32) == 0
    half = levels // 2

    def partial_sums(level):
        filtered = []
        for member in range(mem_dev):
            total = None
            for m in window(level, levels):
                term = band_ref[level, m] * smooth_ref[m // per, member, m % per]
                total = term if total is None else total + term
            filtered.append(total)
        sums = []
        for variable in range(variables):
            total = perturb_ref[0, variable, level] * filtered[0]
            for member in range(1, mem_dev):
                total = total + perturb_ref[member, variable, level] * filtered[member]
            sums.append(total)
        return sums

    for row in range(half):
        lower, upper = partial_sums(row), partial_sums(row + half)
        for variable in range(variables):
            keep_ref[variable, row] = jnp.where(lower_mine, lower[variable], upper[variable])
            give_ref[variable, row] = jnp.where(lower_mine, upper[variable], lower[variable])


def adjoint_kernel(
    levels, mine_ref, other_ref, perturb_ref, count_ref, kind_ref, flag_ref, table_ref, band_ref, out_ref
):
    mem_dev, variables = perturb_ref.shape[:2]
    per = out_ref.shape[2]
    half = levels // 2
    count = count_ref[...].astype(jnp.float32)
    kind = kind_ref[...]
    kinds = table_ref.shape[0]
    masks = [kind == q for q in range(kinds)]
    lower_mine = jnp.full(kind.shape, flag_ref[0], jnp.int32) == 0
    adjoint = {}
    for step in range(levels + HB):
        if step < levels:
            weighted = []
            for variable in range(variables):
                column = variable * levels + step
                looked_up = jnp.full(kind.shape, table_ref[0, column], jnp.float32)
                for q in range(1, kinds):
                    looked_up = jnp.where(masks[q], table_ref[q, column], looked_up)
                mine, other = mine_ref[variable, step % half], other_ref[variable, step % half]
                if step < half:
                    increment = jnp.where(lower_mine, mine, other)
                else:
                    increment = jnp.where(lower_mine, other, mine)
                weighted.append(looked_up * count * increment)
            for member in range(mem_dev):
                total = perturb_ref[member, 0, step] * weighted[0]
                for variable in range(1, variables):
                    total = total + perturb_ref[member, variable, step] * weighted[variable]
                adjoint[member, step] = total
        m = step - HB
        if m >= 0:
            for member in range(mem_dev):
                total = None
                for level in window(m, levels):
                    term = band_ref[level, m] * adjoint[member, level]
                    total = term if total is None else total + term
                out_ref[m // per, member, m % per] = total


def member_sum(devices, keep, give):
    cores = [(d, d ^ 1) for d in range(devices)]
    mine = keep + lax.ppermute(give, "mem", cores)
    pairs = mine
    for shift in range(1, devices // 2):
        step = [(d, (d + 2 * shift) % devices) for d in range(devices)]
        mine = mine + lax.ppermute(pairs, "mem", step)
    return mine, lax.ppermute(mine, "mem", cores)


def local(wide, members, control, perturb, obs_count, obs_kind, obs_table, band_filter, diffusivity):
    mem_dev, lev_dev, nlat, nlon = control.shape
    variables, levels, lat_dev = perturb.shape[1:4]
    east_edge, north_edge = edge_coeffs(diffusivity)
    east_edge, north_edge = east_edge.T, north_edge.T
    control = jnp.swapaxes(control, 2, 3)
    chunk = 2 * LANES
    bounds = [(start, min(start + chunk, nlon)) for start in range(0, nlon, chunk)]
    params = pltpu.CompilerParams(vmem_limit_bytes=VMEM_LIMIT)
    whole = pl.BlockSpec((nlon, nlat), lambda k, l: (0, 0))
    plane = pl.BlockSpec((1, 1, nlon, nlat), lambda k, l: (k, l, 0, 0))
    pieces = [
        pl.BlockSpec((wide, 1, 1, lat_dev, stop - start), lambda k, l: (0, k, l, 0, 0))
        for start, stop in bounds
    ]
    piece_shapes = [
        jax.ShapeDtypeStruct((wide, mem_dev, lev_dev, lat_dev, stop - start), jnp.float32)
        for start, stop in bounds
    ]
    field_bytes = 4 * mem_dev * lev_dev * nlat * nlon
    steps_cost = pl.CostEstimate(
        flops=ITERS * 9 * field_bytes // 4, bytes_accessed=2 * field_bytes, transcendentals=0
    )
    smooth = pl.pallas_call(
        functools.partial(forward_kernel, bounds, chunk),
        grid=(mem_dev, lev_dev),
        in_specs=[whole, whole, plane],
        out_specs=pieces,
        out_shape=piece_shapes,
        scratch_shapes=[pltpu.VMEM((len(bounds) * chunk, nlat), jnp.float32)],
        compiler_params=params,
        cost_estimate=steps_cost,
    )(east_edge, north_edge, control)

    tile = strip_rows(lat_dev)
    smem = pl.BlockSpec(memory_space=pltpu.SMEM)
    flag = (lax.axis_index("mem") % 2).reshape((1,)).astype(jnp.int32)
    moved = []
    for (start, stop), part in zip(bounds, smooth):
        columns = lax.all_to_all(part, "wide", split_axis=0, concat_axis=0)
        size = stop - start
        first = start // LANES
        grid = (lat_dev // tile, -(-size // LANES))
        column_spec = pl.BlockSpec(
            (wide, mem_dev, lev_dev, tile, LANES), lambda i, j: (0, 0, 0, i, j)
        )
        perturb_spec = pl.BlockSpec(
            (mem_dev, variables, levels, tile, LANES),
            lambda i, j, first=first: (0, 0, 0, i, first + j),
        )
        half_spec = pl.BlockSpec((variables, levels // 2, tile, LANES), lambda i, j: (0, 0, i, j))
        half_shape = jax.ShapeDtypeStruct((variables, levels // 2, lat_dev, size), jnp.float32)
        cell_spec = pl.BlockSpec((tile, LANES), lambda i, j, first=first: (i, first + j))
        cells = lat_dev * size * levels
        cost = pl.CostEstimate(
            flops=cells * 60, bytes_accessed=4 * cells * (mem_dev * 4 + 3), transcendentals=0
        )
        keep, give = pl.pallas_call(
            functools.partial(increment_kernel, levels),
            grid=grid,
            in_specs=[column_spec, perturb_spec, smem, smem],
            out_specs=[half_spec, half_spec],
            out_shape=[half_shape, half_shape],
            compiler_params=params,
            cost_estimate=cost,
        )(columns, perturb, band_filter, flag)
        mine, other = member_sum(members, keep, give)
        lifted = pl.pallas_call(
            functools.partial(adjoint_kernel, levels),
            grid=grid,
            in_specs=[half_spec, half_spec, perturb_spec, cell_spec, cell_spec, smem, smem, smem],
            out_specs=column_spec,
            out_shape=jax.ShapeDtypeStruct((wide, mem_dev, lev_dev, lat_dev, size), jnp.float32),
            compiler_params=params,
            cost_estimate=cost,
        )(mine, other, perturb, obs_count, obs_kind, flag, obs_table, band_filter)
        moved.append(lax.all_to_all(lifted, "wide", split_axis=0, concat_axis=0))

    product = pl.pallas_call(
        functools.partial(backward_kernel, bounds),
        grid=(mem_dev, lev_dev),
        in_specs=[whole, whole, plane] + pieces,
        out_specs=plane,
        out_shape=jax.ShapeDtypeStruct(control.shape, jnp.float32),
        scratch_shapes=[
            pltpu.VMEM((nlon, nlat), jnp.float32),
            pltpu.VMEM((nlat, chunk), jnp.float32),
        ],
        compiler_params=params,
        cost_estimate=steps_cost,
    )(east_edge, north_edge, control, *moved)
    return jnp.swapaxes(product, 2, 3)


def solution(mesh):
    placed = (
        P("mem", "wide", None, None),
        P("mem", None, None, "wide", None),
        P("wide", None),
        P("wide", None),
        P(),
        P(),
        P(),
    )
    return jax.shard_map(
        functools.partial(local, mesh.shape["wide"], mesh.shape["mem"]),
        mesh=mesh,
        in_specs=placed,
        out_specs=P("mem", "wide", None, None),
        check_vma=False,
    )
```

time: 826 us -> 528 us (0.64)
  other arithmetic: 251 us -> 8.71 us
  Pallas kernels: 0 us -> 238 us
  local copies, waits for them, and re-layouts: 208 us -> 9.46 us
  waiting for transfers between devices: 286 us -> 139 us
  blocking collectives: 0 us -> 109 us
  matrix products: 29.3 us -> 0 us
  between operations: 14.1 us -> 0.23 us
    pallas_call x0 -> x8, Pallas kernels: none -> 238 us  [the longest x1 101 us: local(): pl.pallas_call(functools.partial(backward_kernel, bounds), grid=(mem_dev,...]
    add x66 -> x6, other arithmetic: 183 us -> 8.53 us  [the longest x3 5.62 us: member_sum(): mine = keep + lax.ppermute(give, 'mem', cores)]
    psum x1 -> x0, waiting for transfers between devices: 168 us -> none  [local(): total_sum = lax.psum(partial_accumulated_sum, 'mem')]
    slice x389 -> x0, local copies, waits for them, and re-layouts: 118 us -> none  [the longest x128 58.2 us: one_step(): flux_east = east_edge * (jnp.roll(field_now, -1, axis=-1) - field_now)]
    all_to_all x0 -> x2, blocking collectives: none -> 109 us  [the longest x1 55.6 us: local(): columns = lax.all_to_all(part, 'wide', split_axis=0, concat_axis=0)]
    ppermute x0 -> x9, waiting for transfers between devices: none -> 89.1 us  [the longest x3 85.3 us: member_sum(): mine = mine + lax.ppermute(pairs, 'mem', step)]
    all_to_all x4, waiting for transfers between devices: 118 us -> 50.2 us  [the longest x2 39.4 us: local(): columns = lax.all_to_all(part, 'wide', split_axis=0, concat_axis=0)]
    while x260 -> x0, local copies, waits for them, and re-layouts: 61.9 us -> none
  transfers between devices with their start and end apart: 5 -> 13, of which waited for: 3 -> 8; matrix products, arithmetic and copies ran while one was open for 22% -> 2% of each run, Pallas kernels for 0% -> 7%
where the time goes in v1:
time: 528 us; the launch traced here: 527 us
  Pallas kernels  238 us (45%)
  waiting for transfers between devices  139 us (26%)
  blocking collectives  109 us (21%)
  starting transfers between devices  22.8 us (4%)
  local copies, waits for them, and re-layouts  9.46 us (2%)
  other arithmetic  8.71 us (2%)
    pallas_call x1, Pallas kernels, local(): pl.pallas_call(functools.partial(backward_kernel, bounds), grid=(mem_dev,...  101 us
    pallas_call x1, Pallas kernels, local(): pl.pallas_call(functools.partial(forward_kernel, bounds, chunk), grid=(me...  101 us
    ppermute x3, waiting for transfers between devices, member_sum(): mine = mine + lax.ppermute(pairs, 'mem', step)  85.3 us
    all_to_all x1, blocking collectives, local(): columns = lax.all_to_all(part, 'wide', split_axis=0, concat_axis=0)  55.6 us
    all_to_all x1, blocking collectives, local(): moved.append(lax.all_to_all(lifted, 'wide', split_axis=0, concat_axis=0))  53.4 us
    all_to_all x2, waiting for transfers between devices, local(): columns = lax.all_to_all(part, 'wide', split_axis=0, concat_axis=0)  39.4 us
    pallas_call x3, Pallas kernels, local(): pl.pallas_call(functools.partial(adjoint_kernel, levels), grid=grid, in_s...  19.3 us
    pallas_call x3, Pallas kernels, local(): pl.pallas_call(functools.partial(increment_kernel, levels), grid=grid, in...  16.3 us
  transfers between devices with their start and end apart: 13, of which 8 were waited for; matrix products, arithmetic and copies ran while one was open for 2% of the time, Pallas kernels for 7%

profile of v1, /device:TPU:0, one launch (start us, length us, event | category | flops | bytes accessed | tf_op | source)
XLA Modules:
  0.0 527.4 jit_solution(13825391413056365135)
XLA Ops:
  0.0 0.8 slice.17
  0.8 1.1 slice.18
  1.9 1.0 slice.16
  2.9 0.2 fusion.4
  3.1 101.0 %shard_map.73 = (f32[8,2,8,16,256]{4,3,2,1,0:T(8,128)S(1)}, f32[8,2,8,16,256]{4,3,2,1,0:T(8,128)S(1)}, f32[8,2,8,16,208]{4,3,2,1,0:T(8,128)}) custom-call(f32[720,128]{1,0:T(8,128)S(1)} %get-tuple-element.24.east_ref, f32[720,128]{1,0:T(8,128)S(1)} %get-tuple-element.23.north_ref, f32[2,8,720,128]{3,2,1,0:T(8,128)} %bitcast.8), custom_call_target="tpu_custom_call" | custom-call | flops 212336640 | bytes 11796480 | tf_op jit(solution)/shard_map/pallas_call | solution.py:199
  104.1 55.6 %all_to_all.30.smooth_ref = f32[8,2,8,16,208]{4,3,2,1,0:T(8,128)} all-to-all(f32[8,2,8,16,208]{4,3,2,1,0:T(8,128)} %get-tuple-element.20), channel_id=1, replica_groups=mesh['mem'=4,'wide'=8] {'wide'}, dimensions={0} | all-to-all | bytes 3407872 | tf_op jit(solution)/shard_map/all_to_all | solution.py:215
  159.8 3.7 all-to-all-start
  163.5 1.6 copy-done.2
  165.1 5.7 %shard_map.78 = (f32[3,32,16,208]{3,2,1,0:T(8,128)S(1)}, f32[3,32,16,208]{3,2,1,0:T(8,128)}) custom-call(f32[8,2,8,16,208]{4,3,2,1,0:T(8,128)S(1)} %copy-done.2, f32[2,3,64,16,720]{4,3,2,1,0:T(8,128)} %perturb_ref.11, f32[64,64]{1,0:T(8,128)S(1)} %copy-done.9, s32[1]{0:T(128)} %bitcast.3.flag_ref), custom_call_target="tpu_custom_call" | custom-call | flops 12779520 | bytes 9371648 | tf_op jit(solution)/shard_map/pallas_call | solution.py:233
  170.8 1.1 copy-done.8
  172.0 39.4 %all-to-all-done.smooth_ref = f32[8,2,8,16,256]{4,3,2,1,0:T(8,128)S(1)} async-done(((f32[8,2,8,16,256]{4,3,2,1,0:T(8,128)}), f32[8,2,8,16,256]{4,3,2,1,0:T(8,128)S(1)}, u32[]{:S(2)}, u32[]{:S(2)}) %all-to-all-start) | async-done | bytes 2097184 | tf_op jit(solution)/shard_map/all_to_all | solution.py:215
  211.4 1.3 copy-done
  212.7 3.6 all-to-all-start.2
  216.3 0.0 copy-start.1
  216.3 2.4 add.35
  218.7 1.6 collective-permute-start.7
  220.3 4.9 shard_map.74
  225.2 0.1 collective-permute-start
  225.3 29.6 %collective-permute-done.7 = f32[3,32,16,208]{3,2,1,0:T(8,128)S(1)} collective-permute-done((f32[3,32,16,208]{3,2,1,0:T(8,128)S(1)}, f32[3,32,16,208]{3,2,1,0:T(8,128)S(1)}, u32[]{:S(2)}, u32[]{:S(2)}) %collective-permute-start.7) | collective-permute-done | bytes 1277984 | tf_op jit(solution)/shard_map/ppermute | solution.py:172
  254.8 0.3 add.36.mine_ref
  255.2 0.1 collective-permute-start.8
  255.3 0.0 copy-start.10
  255.3 0.0 copy-start.11
  255.3 1.5 add.31
  256.8 1.5 collective-permute-start.1
  258.3 0.4 collective-permute-done.8.other_ref
  258.7 6.2 %shard_map.79 = f32[8,2,8,16,208]{4,3,2,1,0:T(8,128)S(1)} custom-call(f32[3,32,16,208]{3,2,1,0:T(8,128)S(1)} %add.36.mine_ref, f32[3,32,16,208]{3,2,1,0:T(8,128)S(1)} %collective-permute-done.8.other_ref, f32[2,3,64,16,720]{4,3,2,1,0:T(8,128)} %perturb_ref.11, s32[16,720]{1,0:T(8,128)S(1)} %copy-done.10, s32[16,720]{1,0:T(8,128)S(1)} %copy-done.11, ...), custom_call_target="tpu_custom_call" | custom-call | flops 12779520 | bytes 9371648 | tf_op jit(solution)/shard_map/pallas_call | solution.py:243
  264.9 1.3 copy-done.3
  266.2 5.7 %all-to-all-start.5 = ((f32[8,2,8,16,208]{4,3,2,1,0:T(8,128)}), f32[8,2,8,16,208]{4,3,2,1,0:T(8,128)}, u32[]{:S(2)}, u32[]{:S(2)}) async-start(f32[8,2,8,16,208]{4,3,2,1,0:T(8,128)} %copy-done.3), calls=%async_computation.5 | async-start | bytes 4194304 | tf_op jit(solution)/shard_map/all_to_all | solution.py:252
  271.9 21.9 %collective-permute-done.1 = f32[3,32,16,256]{3,2,1,0:T(8,128)} collective-permute-done((f32[3,32,16,256]{3,2,1,0:T(8,128)}, f32[3,32,16,256]{3,2,1,0:T(8,128)}, u32[]{:S(2)}, u32[]{:S(2)}) %collective-permute-start.1) | collective-permute-done | bytes 1572896 | tf_op jit(solution)/shard_map/ppermute | solution.py:172
  293.9 2.2 add.32.mine_ref
  296.1 0.1 collective-permute-start.2
  296.2 5.7 %shard_map.76 = (f32[3,32,16,256]{3,2,1,0:T(8,128)S(1)}, f32[3,32,16,256]{3,2,1,0:T(8,128)}) custom-call(f32[8,2,8,16,256]{4,3,2,1,0:T(8,128)S(1)} %all-to-all-done.2.smooth_ref, f32[2,3,64,16,720]{4,3,2,1,0:T(8,128)} %perturb_ref.11, f32[64,64]{1,0:T(8,128)S(1)} %copy-done.9, s32[1]{0:T(128)} %bitcast.3.flag_ref), custom_call_target="tpu_custom_call" | custom-call | flops 15728640 | bytes 11534336 | tf_op jit(solution)/shard_map/pallas_call | solution.py:233
  301.9 1.1 copy-done.6
  303.0 0.5 collective-permute-start.3
  303.5 6.9 %shard_map.75 = f32[8,2,8,16,256]{4,3,2,1,0:T(8,128)} custom-call(f32[3,32,16,256]{3,2,1,0:T(8,128)S(1)} %add.32.mine_ref, f32[3,32,16,256]{3,2,1,0:T(8,128)S(1)} %collective-permute-done.2.other_ref, f32[2,3,64,16,720]{4,3,2,1,0:T(8,128)} %perturb_ref.11, s32[16,720]{1,0:T(8,128)S(1)} %copy-done.10, s32[16,720]{1,0:T(8,128)S(1)} %copy-done.11, ...), custom_call_target="tpu_custom_call" | custom-call | flops 15728640 | bytes 11534336 | tf_op jit(solution)/shard_map/pallas_call | solution.py:243
  310.4 10.2 %all-to-all-done.5.rest_2_ = f32[8,2,8,16,208]{4,3,2,1,0:T(8,128)} async-done(((f32[8,2,8,16,208]{4,3,2,1,0:T(8,128)}), f32[8,2,8,16,208]{4,3,2,1,0:T(8,128)}, u32[]{:S(2)}, u32[]{:S(2)}) %all-to-all-start.5) | async-done | bytes 1703968 | tf_op jit(solution)/shard_map/all_to_all | solution.py:252
  320.6 4.3 all-to-all-start.1
  324.9 1.8 add.33
  326.7 1.6 collective-permute-start.4
  328.3 33.8 %collective-permute-done.4 = f32[3,32,16,256]{3,2,1,0:T(8,128)S(1)} collective-permute-done((f32[3,32,16,256]{3,2,1,0:T(8,128)S(1)}, f32[3,32,16,256]{3,2,1,0:T(8,128)S(1)}, u32[]{:S(2)}, u32[]{:S(2)}) %collective-permute-start.4) | collective-permute-done | bytes 1572896 | tf_op jit(solution)/shard_map/ppermute | solution.py:172
  362.1 0.3 add.34.mine_ref
  362.4 0.1 collective-permute-start.5
  362.5 3.4 collective-permute-done.5.other_ref
  365.9 6.2 %shard_map.77 = f32[8,2,8,16,256]{4,3,2,1,0:T(8,128)S(1)} custom-call(f32[3,32,16,256]{3,2,1,0:T(8,128)S(1)} %add.34.mine_ref, f32[3,32,16,256]{3,2,1,0:T(8,128)S(1)} %collective-permute-done.5.other_ref, f32[2,3,64,16,720]{4,3,2,1,0:T(8,128)} %perturb_ref.11, s32[16,720]{1,0:T(8,128)S(1)} %copy-done.10, s32[16,720]{1,0:T(8,128)S(1)} %copy-done.11, ...), custom_call_target="tpu_custom_call" | custom-call | flops 15728640 | bytes 11534336 | tf_op jit(solution)/shard_map/pallas_call | solution.py:243
  372.1 0.6 all-to-all-done.1.rest_0_
  372.7 53.4 %all_to_all.31.rest_1_ = f32[8,2,8,16,256]{4,3,2,1,0:T(8,128)S(1)} all-to-all(f32[8,2,8,16,256]{4,3,2,1,0:T(8,128)S(1)} %shard_map.77), channel_id=1, replica_groups=mesh['mem'=4,'wide'=8] {'wide'}, dimensions={0} | all-to-all | bytes 4194304 | tf_op jit(solution)/shard_map/all_to_all | solution.py:252
  426.1 101.3 %shard_map.80 = f32[2,8,720,128]{3,2,1,0:T(8,128)} custom-call(f32[720,128]{1,0:T(8,128)S(1)} %get-tuple-element.24.east_ref, f32[720,128]{1,0:T(8,128)S(1)} %get-tuple-element.23.north_ref, f32[2,8,720,128]{3,2,1,0:T(8,128)} %bitcast.9, f32[8,2,8,16,256]{4,3,2,1,0:T(8,128)} %all-to-all-done.1.rest_0_, f32[8,2,8,16,256]{4,3,2,1,0:T(8,128)S(1)} %all_to_all.31.rest_1_, ...), custom_call_target="tpu_custom_call" | custom-call | flops 212336640 | bytes 11796480 | tf_op jit(solution)/shard_map/pallas_call | solution.py:254
  (27 shorter events, 0.1 us)
Async XLA Ops:
  0.0 2.9 copy-start.13
  104.1 55.6 %copy-start.4 = (f32[8,2,8,16,256]{4,3,2,1,0:T(8,128)}, f32[8,2,8,16,256]{4,3,2,1,0:T(8,128)S(1)}, u32[]{:S(2)}) copy-start(f32[8,2,8,16,256]{4,3,2,1,0:T(8,128)S(1)} %get-tuple-element.17) | copy-start | bytes 6291460
  104.1 55.6 %copy-start.5 = (f32[8,2,8,16,256]{4,3,2,1,0:T(8,128)}, f32[8,2,8,16,256]{4,3,2,1,0:T(8,128)S(1)}, u32[]{:S(2)}) copy-start(f32[8,2,8,16,256]{4,3,2,1,0:T(8,128)S(1)} %get-tuple-element.14) | copy-start | bytes 6291460
  159.8 3.8 copy-start.9
  159.8 51.6 %all-to-all-start = ((f32[8,2,8,16,256]{4,3,2,1,0:T(8,128)}), f32[8,2,8,16,256]{4,3,2,1,0:T(8,128)S(1)}, u32[]{:S(2)}, u32[]{:S(2)}) async-start(f32[8,2,8,16,256]{4,3,2,1,0:T(8,128)} %copy-done.5), calls=%async_computation | async-start | bytes 4194304 | tf_op jit(solution)/shard_map/all_to_all | solution.py:215
  163.5 1.6 copy-start.2
  170.8 1.1 copy-start.8
  172.0 44.4 %collective-permute-start.6 = (f32[3,32,16,208]{3,2,1,0:T(8,128)}, f32[3,32,16,208]{3,2,1,0:T(8,128)}, u32[]{:S(2)}, u32[]{:S(2)}) collective-permute-start(f32[3,32,16,208]{3,2,1,0:T(8,128)} %get-tuple-element.22), channel_id=1, source_target_pairs={{0,8},{8,0},{16,24},{24,16},{1,9},{9,1},{17,25},{25,17},{2,10},{10... | collective-permute-start | bytes 3833864 | tf_op jit(solution)/shard_map/ppermute | solution.py:168
  211.4 1.3 copy-start
  212.7 53.5 %all-to-all-start.2 = ((f32[8,2,8,16,256]{4,3,2,1,0:T(8,128)}), f32[8,2,8,16,256]{4,3,2,1,0:T(8,128)S(1)}, u32[]{:S(2)}, u32[]{:S(2)}) async-start(f32[8,2,8,16,256]{4,3,2,1,0:T(8,128)} %copy-done.4), calls=%async_computation.2 | async-start | bytes 4194304 | tf_op jit(solution)/shard_map/all_to_all | solution.py:215
  216.3 3.9 copy-start.1
  218.7 36.1 %collective-permute-start.7 = (f32[3,32,16,208]{3,2,1,0:T(8,128)S(1)}, f32[3,32,16,208]{3,2,1,0:T(8,128)S(1)}, u32[]{:S(2)}, u32[]{:S(2)}) collective-permute-start(f32[3,32,16,208]{3,2,1,0:T(8,128)S(1)} %add.35), channel_id=1, source_target_pairs={{0,16},{8,24},{16,0},{24,8},{1,17},{9,25},{17,1},{25,9},{2,18},{10... | collective-permute-start | bytes 3833864 | tf_op jit(solution)/shard_map/ppermute | solution.py:172
  225.2 30.1 %collective-permute-start = (f32[3,32,16,256]{3,2,1,0:T(8,128)S(1)}, f32[3,32,16,256]{3,2,1,0:T(8,128)S(1)}, u32[]{:S(2)}, u32[]{:S(2)}) collective-permute-start(f32[3,32,16,256]{3,2,1,0:T(8,128)S(1)} %get-tuple-element.16), channel_id=1, source_target_pairs={{0,8},{8,0},{16,24},{24,16},{1,9},{9,1},{17,25},{25,17},{2,10},{10... | collective-permute-start | bytes 4718600 | tf_op jit(solution)/shard_map/ppermute | solution.py:168
  255.2 3.5 collective-permute-start.8
  255.3 3.4 copy-start.10
  255.3 3.4 copy-start.11
  255.3 3.4 copy-start.12
  256.8 37.1 %collective-permute-start.1 = (f32[3,32,16,256]{3,2,1,0:T(8,128)}, f32[3,32,16,256]{3,2,1,0:T(8,128)}, u32[]{:S(2)}, u32[]{:S(2)}) collective-permute-start(f32[3,32,16,256]{3,2,1,0:T(8,128)} %add.31), channel_id=1, source_target_pairs={{0,16},{8,24},{16,0},{24,8},{1,17},{9,25},{17,1},{25,9},{2,18},{10... | collective-permute-start | bytes 4718600 | tf_op jit(solution)/shard_map/ppermute | solution.py:172
  264.9 1.3 copy-start.3
  266.2 54.3 %all-to-all-start.5 = ((f32[8,2,8,16,208]{4,3,2,1,0:T(8,128)}), f32[8,2,8,16,208]{4,3,2,1,0:T(8,128)}, u32[]{:S(2)}, u32[]{:S(2)}) async-start(f32[8,2,8,16,208]{4,3,2,1,0:T(8,128)} %copy-done.3), calls=%async_computation.5 | async-start | bytes 4194304 | tf_op jit(solution)/shard_map/all_to_all | solution.py:252
  296.1 7.4 %collective-permute-start.2 = (f32[3,32,16,256]{3,2,1,0:T(8,128)S(1)}, f32[3,32,16,256]{3,2,1,0:T(8,128)S(1)}, u32[]{:S(2)}, u32[]{:S(2)}) collective-permute-start(f32[3,32,16,256]{3,2,1,0:T(8,128)S(1)} %add.32.mine_ref), channel_id=1, source_target_pairs={{0,8},{8,0},{16,24},{24,16},{1,9},{9,1},{17,25},{25,17},{2,10},{10... | collective-permute-start | bytes 4718600 | tf_op jit(solution)/shard_map/ppermute | solution.py:173
  301.9 1.1 copy-start.6
  303.0 21.9 %collective-permute-start.3 = (f32[3,32,16,256]{3,2,1,0:T(8,128)}, f32[3,32,16,256]{3,2,1,0:T(8,128)}, u32[]{:S(2)}, u32[]{:S(2)}) collective-permute-start(f32[3,32,16,256]{3,2,1,0:T(8,128)} %get-tuple-element.19), channel_id=1, source_target_pairs={{0,8},{8,0},{16,24},{24,16},{1,9},{9,1},{17,25},{25,17},{2,10},{10... | collective-permute-start | bytes 4718600 | tf_op jit(solution)/shard_map/ppermute | solution.py:168
  310.4 14.5 %copy-start.7 = (f32[3,32,16,256]{3,2,1,0:T(8,128)S(1)}, f32[3,32,16,256]{3,2,1,0:T(8,128)}, u32[]{:S(2)}) copy-start(f32[3,32,16,256]{3,2,1,0:T(8,128)} %copy-done.6) | copy-start | bytes 4718596
  320.6 52.2 %all-to-all-start.1 = ((f32[8,2,8,16,256]{4,3,2,1,0:T(8,128)}), f32[8,2,8,16,256]{4,3,2,1,0:T(8,128)}, u32[]{:S(2)}, u32[]{:S(2)}) async-start(f32[8,2,8,16,256]{4,3,2,1,0:T(8,128)} %shard_map.75), calls=%async_computation.1 | async-start | bytes 4194304 | tf_op jit(solution)/shard_map/all_to_all | solution.py:252
  326.7 35.4 %collective-permute-start.4 = (f32[3,32,16,256]{3,2,1,0:T(8,128)S(1)}, f32[3,32,16,256]{3,2,1,0:T(8,128)S(1)}, u32[]{:S(2)}, u32[]{:S(2)}) collective-permute-start(f32[3,32,16,256]{3,2,1,0:T(8,128)S(1)} %add.33), channel_id=1, source_target_pairs={{0,16},{8,24},{16,0},{24,8},{1,17},{9,25},{17,1},{25,9},{2,18},{10... | collective-permute-start | bytes 4718600 | tf_op jit(solution)/shard_map/ppermute | solution.py:172
  362.4 3.5 collective-permute-start.5
